TPU v7x, 32 devices: a whole 2x2x4 slice. The times are simulated.
32 devices in a mesh: pw: 16 (over z, y, core), band: 2 (over x).
Axes of the slice: x: 2, y: 2, z: 4, core: 2. Of those that a mesh axis runs over, the one named last changes fastest.
Arguments:
- waves: bfloat16 [2, 20480, 1792], P(None, 'pw', 'band'), may hold values from -6 to 6
- projectors: bfloat16 [2, 128, 20480], P(None, 'band', 'pw'), may hold values from -0.03125 to 0.03125
- coupling: float32 [12, 13, 13], replicated, may hold values from -22.768398 to 22.768398
- offsets: int32 [12], replicated, may hold values from 0 to 119, as said below
- counts: int32 [12], replicated, may hold values from 9 to 13, as said below
Outputs:
- applied: bfloat16 [2, 20480, 1792], P(None, 'pw', 'band')
Inputs may be any that keep to these rules, and one draw needn't show every extreme that they name: `counts`: each atom has 9 or 13 projectors, exactly 5 atoms have 13, so the atoms fill all 128 projectors. offsets are the running sums of counts before each atom, so atoms take consecutive projectors in order.
All inputs are finite; a program needn't handle non-finite values.
Results may differ from a plain program's by a relative error of at most 0.0049.
Values may be sent and summed in bfloat16 or wider, within the bound.
A program may use at most 64 MiB of HBM per device.

v0:
```python
import jax
import jax.numpy as jnp
from jax import lax
from jax.sharding import PartitionSpec as P

NP = 128
M = 13


def coupling_block(coupling, offsets, counts):
    proj = jnp.arange(NP, dtype=jnp.int32)
    local = jnp.arange(M, dtype=jnp.int32)
    target = offsets[:, None] + local[None, :]
    select = (proj[None, :, None] == target[:, None, :]) & (
        local[None, None, :] < counts[:, None, None]
    )
    select = select.astype(jnp.float32)
    sym = (coupling + jnp.swapaxes(coupling, 1, 2)) * 0.5
    return jnp.einsum("api,aij,aqj->pq", select, sym, select, precision=lax.Precision.HIGHEST)


def project(rows, waves):
    real = jnp.dot(rows[0], waves[0], preferred_element_type=jnp.float32) + jnp.dot(
        rows[1], waves[1], preferred_element_type=jnp.float32
    )
    imag = jnp.dot(rows[0], waves[1], preferred_element_type=jnp.float32) - jnp.dot(
        rows[1], waves[0], preferred_element_type=jnp.float32
    )
    return jnp.stack([real, imag])


def spread_back(rows, coupled):
    dims = (((0,), (0,)), ((), ()))
    real = lax.dot_general(
        rows[0], coupled[0], dims, preferred_element_type=jnp.float32
    ) - lax.dot_general(rows[1], coupled[1], dims, preferred_element_type=jnp.float32)
    imag = lax.dot_general(
        rows[0], coupled[1], dims, preferred_element_type=jnp.float32
    ) + lax.dot_general(rows[1], coupled[0], dims, preferred_element_type=jnp.float32)
    return jnp.stack([real, imag])


def shards(waves, projectors, coupling, offsets, counts):
    block = coupling_block(coupling, offsets, counts)
    gathered = lax.all_gather(projectors, "band", axis=1, tiled=True)
    partial_coeffs = project(gathered, waves)
    coeffs = lax.psum(partial_coeffs, "pw")
    coupled = jnp.einsum("pq,kqb->kpb", block, coeffs, precision=lax.Precision.HIGHEST).astype(
        jnp.bfloat16
    )
    result = spread_back(gathered, coupled)
    return result.astype(jnp.bfloat16)


def solution(mesh):
    placed = (P(None, "pw", "band"), P(None, "band", "pw"), P(), P(), P())
    return jax.shard_map(
        shards, mesh=mesh, in_specs=placed, out_specs=P(None, "pw", "band"), check_vma=False
    )
```

profile of v0, /device:TPU:1, one launch (start us, length us, event | category | flops | bytes accessed | tf_op | source)
XLA Modules:
  0.0 140.4 jit_solution(7559047400933185581)
XLA Ops:
  6.5 0.0 all-reduce.2.cloned.1.call-start
  6.5 0.0 copy-start.3
  6.5 10.5 %all_gather.3 = bf16[2,128,1280]{2,1,0:T(8,128)(2,1)S(1)} all-gather(bf16[2,64,1280]{2,1,0:T(8,128)(2,1)} %param.6), channel_id=1, replica_groups=mesh['pw'=16,'band'=2] {'band'}, dimensions={1}, use_global_device_ids=true | all-gather | bytes 983040 | tf_op jit(solution)/shard_map/all_gather | solution.py:45
  17.0 2.2 %fusion.2 = f32[128,896]{1,0:T(8,128)S(1)} fusion(bf16[2,1280,896]{2,1,0:T(8,128)(2,1)} %param.5, bf16[2,128,1280]{2,1,0:T(8,128)(2,1)S(1)} %all_gather.3), kind=kOutput, calls=%fused_computation.5 | convolution fusion | flops 293601280 | bytes 3080192 | tf_op jit(solution)/shard_map/dot_general | solution.py:26
  19.2 2.2 %fusion.4 = f32[128,896]{1,0:T(8,128)S(1)} fusion(bf16[2,1280,896]{2,1,0:T(8,128)(2,1)} %param.5, bf16[2,128,1280]{2,1,0:T(8,128)(2,1)S(1)} %all_gather.3), kind=kOutput, calls=%fused_computation.7 | convolution fusion | flops 293601280 | bytes 3080192 | tf_op jit(solution)/shard_map/dot_general | solution.py:23
  21.4 0.0 copy-done.3
  21.4 0.0 copy-start.1
  21.4 0.0 copy-start.2
  21.4 0.0 copy-start
  21.4 0.5 fusion.24
  21.9 0.5 fusion.18
  22.4 1.0 pad_maximum_fusion.1
  23.4 0.0 all-reduce.2.cloned.1.call-update
  23.4 0.0 copy-done.1
  23.5 0.1 iota_compare_fusion.1
  23.5 0.0 copy-done.2
  23.5 0.1 iota_add_fusion
  23.6 0.0 copy-done
  23.6 0.2 copy.6
  23.8 0.8 fusion.30
  24.5 0.8 fusion.28
  25.4 92.7 %all-reduce.2.cloned.1.call-done = f32[2,128,896]{2,1,0:T(8,128)} async-done(((f32[2,128,896]{2,1,0:T(8,128)}), f32[2,128,896]{2,1,0:T(8,128)}) %all-reduce.2.cloned.1.call-update) | async-done | bytes 917520 | tf_op jit(solution)/shard_map/psum | solution.py:47
  118.0 2.8 %fusion.14 = bf16[2,128,896]{1,2,0:T(8,128)(2,1)S(1)} fusion(f32[2,128,896]{2,1,0:T(8,128)} %all-reduce.2.cloned.1.call-done, f32[128,128,1]{1,0,2:T(8,128)S(1)} %fusion.28), kind=kOutput, calls=%fused_computation.18 | convolution fusion | flops 352550912 | bytes 1441792 | tf_op jit(solution)/shard_map/pq,kqb->kpb/dot_general | solution.py:48
  120.8 0.7 fusion.36
  121.5 0.7 fusion.37
  122.3 0.8 fusion.1
  123.1 0.8 fusion
  123.8 2.5 %pad_maximum_fusion = bf16[2,1280,896]{1,2,0:T(8,128)(2,1)} fusion(bf16[1,1280,896]{1,2,0:T(8,128)(2,1)S(1)} %fusion.1, bf16[1,1280,896]{1,2,0:T(8,128)(2,1)S(1)} %fusion), kind=kLoop, calls=%fused_computation | loop fusion | flops 2293760 | bytes 9175040 | tf_op jit(solution)/shard_map/stack | solution.py:40
  126.3 7.3 %copy.8 = bf16[2,1280,896]{2,1,0:T(8,128)(2,1)} copy(bf16[2,1280,896]{1,2,0:T(8,128)(2,1)} %pad_maximum_fusion) | data formatting | bytes 9175040 | tf_op jit(solution)/shard_map/stack | solution.py:40
Async XLA Ops:
  6.5 111.5 %all-reduce.2.cloned.1.call-start = ((), (), s32[]{:S(2)}) async-start(), calls=%async_computation | async-start | bytes 1835008 | tf_op jit(solution)/shard_map/psum | solution.py:47
  6.5 14.8 %copy-start.3 = (bf16[2,1280,896]{2,1,0:T(8,128)(2,1)S(1)}, bf16[2,1280,896]{2,1,0:T(8,128)(2,1)}, u32[]{:S(2)}) copy-start(bf16[2,1280,896]{2,1,0:T(8,128)(2,1)} %param.5) | copy-start | bytes 13762564
  21.4 2.1 %copy-start.1 = (s32[12]{0:T(128)S(1)}, s32[12]{0:T(128)}, u32[]{:S(2)}) copy-start(s32[12]{0:T(128)} %param.9) | copy-start | bytes 148
  21.4 2.2 %copy-start.2 = (s32[12]{0:T(128)S(1)}, s32[12]{0:T(128)}, u32[]{:S(2)}) copy-start(s32[12]{0:T(128)} %param.8) | copy-start | bytes 148
  21.4 2.2 %copy-start = (f32[12,13,13]{2,1,0:T(8,128)S(1)}, f32[12,13,13]{2,1,0:T(8,128)}, u32[]{:S(2)}) copy-start(f32[12,13,13]{2,1,0:T(8,128)} %param.7) | copy-start | bytes 24340
Sparse Core Ops, SparseCore 0:
  23.6 94.4 all-reduce.1
where the time goes:
time: 141 us; the launch traced here: 140 us
  waiting for transfers between devices  92.7 us (66%)
  between operations  13.5 us (10%)
  matrix products  12.7 us (9%)
  blocking collectives  10.5 us (7%)
  local copies, waits for them, and re-layouts  7.46 us (5%)
  other arithmetic  3.59 us (3%)
    psum x1, waiting for transfers between devices, shards(): coeffs = lax.psum(partial_coeffs, 'pw')  92.7 us
    all_gather x1, blocking collectives, shards(): gathered = lax.all_gather(projectors, 'band', axis=1, tiled=True)  10.5 us
    another operation x1, local copies, waits for them, and re-layouts, spread_back(): return jnp.stack([real, imag])  7.27 us
  transfers between devices with their start and end apart: 1, of which 1 were waited for; matrix products, arithmetic and copies ran while one was open for 1% of the time, Pallas kernels for 0%

commit v1 on v0

v1 whole, which is shorter than its diff:
```python
import functools

import jax
import jax.numpy as jnp
from jax import lax
from jax.experimental import pallas as pl
from jax.experimental.pallas import tpu as pltpu
from jax.sharding import PartitionSpec as P

NP = 128
M = 13
LANES = 128
MESH = pl.DeviceIdType.MESH


def coupling_block(coupling, offsets, counts):
    proj = jnp.arange(NP, dtype=jnp.int32)
    local = jnp.arange(M, dtype=jnp.int32)
    target = offsets[:, None] + local[None, :]
    select = (proj[None, :, None] == target[:, None, :]) & (
        local[None, None, :] < counts[:, None, None]
    )
    select = select.astype(jnp.float32)
    sym = (coupling + jnp.swapaxes(coupling, 1, 2)) * 0.5
    return jnp.einsum("api,aij,aqj->pq", select, sym, select, precision=lax.Precision.HIGHEST)


def column_tiles(columns):
    return [(start, min(256, columns - start)) for start in range(0, columns, 256)]


def gather_kernel(n_pw, n_band, waves, proj, block, pt_out, c_out,
                  w, p_all, acc, sib, send, recv, total, c_all, pt,
                  w_sem, own_sem, out_sem, p_send, p_recv, s_send, s_recv,
                  r_send, r_recv, g_send, g_recv, f_send, f_recv):
    pw = lax.axis_index("pw")
    band = lax.axis_index("band")
    chip, core = lax.div(pw, 2), lax.rem(pw, 2)
    chips = n_pw // 2
    held = proj.shape[1]
    columns = waves.shape[2]
    blocks = columns // LANES
    piece = min(32, held)
    tiles = column_tiles(columns)
    sibling = (chip * 2 + 1 - core, band)

    def chip_at(step):
        return lax.rem(chip + step, chips)

    def same_core(other):
        return (other * 2 + core, band)

    wave_copies = []
    for t, (start, size) in enumerate(tiles):
        copy = pltpu.make_async_copy(
            waves.at[:, :, pl.ds(start, size)], w.at[:, :, pl.ds(start, size)], w_sem.at[t])
        copy.start()
        wave_copies.append(copy)
    own_rows = pl.multiple_of(band * held, held)
    own = pltpu.make_async_copy(proj, p_all.at[:, pl.ds(own_rows, held), :], own_sem.at[0])
    own.start()

    barrier = pltpu.get_barrier_semaphore()
    for d in range(1, n_band):
        pl.semaphore_signal(barrier, inc=1, device_id=(pw, lax.rem(band + d, n_band)), device_id_type=MESH)
    pl.semaphore_signal(barrier, inc=1, device_id=sibling, device_id_type=MESH)
    for d in range(1, chips):
        pl.semaphore_signal(barrier, inc=1, device_id=same_core(chip_at(d)), device_id_type=MESH)
    pl.semaphore_wait(barrier, n_band - 1 + 1 + chips - 1)

    p_copies = {}
    for d in range(1, n_band):
        for s in range(held // piece):
            rows = pl.ds(pl.multiple_of(band * held + s * piece, piece), piece)
            copy = pltpu.make_async_remote_copy(
                src_ref=proj.at[:, pl.ds(s * piece, piece), :],
                dst_ref=p_all.at[:, rows, :],
                send_sem=p_send.at[d - 1, s], recv_sem=p_recv.at[d - 1, s],
                device_id=(pw, lax.rem(band + d, n_band)), device_id_type=MESH)
            copy.start()
            p_copies[d, s] = copy

    def project(row, size, first):
        rows = pl.ds(row, size)
        p0, p1 = p_all[0, rows, :], p_all[1, rows, :]
        lhs0 = jnp.concatenate([p0, -p1], axis=0)
        lhs1 = jnp.concatenate([p1, p0], axis=0)
        for t, (start, width) in enumerate(tiles):
            if first:
                wave_copies[t].wait()
            cols = pl.ds(start, width)
            r = jnp.dot(lhs0, w[0, :, cols], preferred_element_type=jnp.float32)
            r += jnp.dot(lhs1, w[1, :, cols], preferred_element_type=jnp.float32)
            acc[0, rows, cols] = r[:size]
            acc[1, rows, cols] = r[size:]

    sends = []

    def reduce_piece(i, row, size):
        rows = pl.ds(row, size)
        copy = pltpu.make_async_remote_copy(
            src_ref=acc.at[1 - core, rows, :], dst_ref=sib.at[rows, :],
            send_sem=s_send.at[i], recv_sem=s_recv.at[i],
            device_id=sibling, device_id_type=MESH)
        copy.start()
        copy.wait_recv()
        sends.append((None, copy))
        for b in range(blocks):
            cols = pl.ds(b * LANES, LANES)
            send[b, rows, :] = (acc[core, rows, cols] + sib[rows, cols]).astype(jnp.bfloat16)
        for d in range(1, chips):
            other = chip_at(d)

            @pl.when(other < blocks)
            def _():
                reduce_copy(i, d, row, size).start()
            sends.append((other < blocks, reduce_copy(i, d, row, size)))

    def reduce_copy(i, d, row, size):
        other = chip_at(d)
        return pltpu.make_async_remote_copy(
            src_ref=send.at[lax.min(other, blocks - 1), pl.ds(row, size), :],
            dst_ref=recv.at[chip, pl.ds(row, size), :],
            send_sem=r_send.at[i, d], recv_sem=r_recv.at[i, chip],
            device_id=same_core(other), device_id_type=MESH)

    pieces = [(own_rows, held)]
    own.wait()
    project(own_rows, held, True)
    reduce_piece(0, own_rows, held)
    for d in range(1, n_band):
        source = lax.rem(band + n_band - d, n_band)
        for s in range(held // piece):
            p_copies[d, s].wait_recv()
            row = pl.multiple_of(source * held + s * piece, piece)
            project(row, piece, False)
            reduce_piece(len(pieces), row, piece)
            pieces.append((row, piece))

    pt[:, :NP] = p_all[0].T
    pt[:, NP:] = p_all[1].T
    pt_copy = pltpu.make_async_copy(pt, pt_out, out_sem.at[0])
    pt_copy.start()

    def gather_copy(b, d):
        return pltpu.make_async_remote_copy(
            src_ref=c_all.at[core, b], dst_ref=c_all.at[core, b],
            send_sem=g_send.at[d], recv_sem=g_recv.at[b],
            device_id=same_core(chip_at(d)), device_id_type=MESH)

    def forward_copy(k, b):
        return pltpu.make_async_remote_copy(
            src_ref=c_all.at[k, b], dst_ref=c_all.at[k, b],
            send_sem=f_send.at[b], recv_sem=f_recv.at[b],
            device_id=sibling, device_id_type=MESH)

    @pl.when(chip < blocks)
    def _():
        for i, (row, size) in enumerate(pieces):
            rows = pl.ds(row, size)
            value = send[chip, rows, :].astype(jnp.float32)
            for d in range(1, chips):
                source = chip_at(d)
                pltpu.make_async_remote_copy(
                    src_ref=send.at[0, rows, :], dst_ref=recv.at[source, rows, :],
                    send_sem=r_send.at[i, d], recv_sem=r_recv.at[i, source],
                    device_id=same_core(source), device_id_type=MESH).wait_recv()
                value += recv[source, rows, :].astype(jnp.float32)
            total[rows, :] = value
        c_all[core, chip] = jnp.dot(
            block[...], total[...], precision=lax.Precision.HIGHEST,
            preferred_element_type=jnp.float32).astype(jnp.bfloat16)
        for d in range(1, chips):
            gather_copy(chip, d).start()
        forward_copy(core, chip).start()

    for d in range(1, chips):
        source = chip_at(d)

        @pl.when(source < blocks)
        def _():
            gather_copy(source, d).wait_recv()
            forward_copy(core, source).start()

    for b in range(blocks):
        forward_copy(1 - core, b).wait_recv()
    c_copy = pltpu.make_async_copy(c_all, c_out, out_sem.at[1])
    c_copy.start()

    for copy in p_copies.values():
        copy.wait_send()
    for wanted, copy in sends:
        if wanted is None:
            copy.wait_send()
        else:
            pl.when(wanted)(copy.wait_send)

    @pl.when(chip < blocks)
    def _():
        for d in range(1, chips):
            gather_copy(chip, d).wait_send()
    for b in range(blocks):
        forward_copy(core, b).wait_send()
    pt_copy.wait()
    c_copy.wait()


def gather_coupled(n_pw, n_band, waves, projectors, block):
    _, depth, columns = waves.shape
    held = projectors.shape[1]
    chips = n_pw // 2
    blocks = columns // LANES
    subs = held // min(32, held)
    pieces = 1 + (n_band - 1) * subs
    bf16, f32 = jnp.bfloat16, jnp.float32
    dma = pltpu.SemaphoreType.DMA
    hbm = pl.BlockSpec(memory_space=pl.ANY)
    return pl.pallas_call(
        functools.partial(gather_kernel, n_pw, n_band),
        out_shape=[
            jax.ShapeDtypeStruct((depth, 2 * NP), bf16),
            jax.ShapeDtypeStruct((2, blocks, NP, LANES), bf16),
        ],
        in_specs=[hbm, hbm, pl.BlockSpec(memory_space=pltpu.VMEM)],
        out_specs=[hbm, hbm],
        scratch_shapes=[
            pltpu.VMEM((2, depth, columns), bf16),
            pltpu.VMEM((2, NP, depth), bf16),
            pltpu.VMEM((2, NP, columns), f32),
            pltpu.VMEM((NP, columns), f32),
            pltpu.VMEM((blocks, NP, LANES), bf16),
            pltpu.VMEM((chips, NP, LANES), bf16),
            pltpu.VMEM((NP, LANES), f32),
            pltpu.VMEM((2, blocks, NP, LANES), bf16),
            pltpu.VMEM((depth, 2 * NP), bf16),
            dma((len(column_tiles(columns)),)), dma((1,)), dma((2,)),
            dma((n_band - 1, subs)), dma((n_band - 1, subs)),
            dma((pieces,)), dma((pieces,)),
            dma((pieces, chips)), dma((pieces, chips)),
            dma((chips,)), dma((blocks,)),
            dma((blocks,)), dma((blocks,)),
        ],
        compiler_params=pltpu.CompilerParams(
            collective_id=0, has_side_effects=True, vmem_limit_bytes=40 * 2**20),
        name="gather_coupled",
    )(waves, projectors, block)


def spread_kernel(pt, c, out):
    c0, c1 = c[0, 0], c[1, 0]
    rhs = jnp.concatenate(
        [jnp.concatenate([c0, c1], axis=1), jnp.concatenate([-c1, c0], axis=1)], axis=0)
    r = jnp.dot(pt[...], rhs, preferred_element_type=jnp.float32)
    out[0] = r[:, :LANES].astype(out.dtype)
    out[1] = r[:, LANES:].astype(out.dtype)


def spread_back(pt, coupled):
    depth = pt.shape[0]
    blocks = coupled.shape[1]
    return pl.pallas_call(
        spread_kernel,
        grid=(blocks,),
        out_shape=jax.ShapeDtypeStruct((2, depth, blocks * LANES), jnp.bfloat16),
        in_specs=[
            pl.BlockSpec((depth, 2 * NP), lambda b: (0, 0)),
            pl.BlockSpec((2, 1, NP, LANES), lambda b: (0, b, 0, 0)),
        ],
        out_specs=pl.BlockSpec((2, depth, LANES), lambda b: (0, 0, b)),
        compiler_params=pltpu.CompilerParams(vmem_limit_bytes=32 * 2**20),
        name="spread_back",
    )(pt, coupled)


def solution(mesh):
    n_pw, n_band = mesh.shape["pw"], mesh.shape["band"]

    def shards(waves, projectors, coupling, offsets, counts):
        block = coupling_block(coupling, offsets, counts)
        pt, coupled = gather_coupled(n_pw, n_band, waves, projectors, block)
        return spread_back(pt, coupled)

    placed = (P(None, "pw", "band"), P(None, "band", "pw"), P(), P(), P())
    return jax.shard_map(
        shards, mesh=mesh, in_specs=placed, out_specs=P(None, "pw", "band"), check_vma=False
    )
```

time: 141 us -> 41.5 us (0.29)
  waiting for transfers between devices: 92.7 us -> 0 us
  Pallas kernels: 0 us -> 33.8 us
  between operations: 13.5 us -> 0.03 us
  matrix products: 12.7 us -> 1.59 us
  blocking collectives: 10.5 us -> 0 us
  local copies, waits for them, and re-layouts: 7.46 us -> 4.31 us
  other arithmetic: 3.59 us -> 1.45 us
    psum x1 -> x0, waiting for transfers between devices: 92.7 us -> none  [shards(): coeffs = lax.psum(partial_coeffs, 'pw')]
    pallas_call x0 -> x2, Pallas kernels: none -> 33.8 us  [the longest x1 29 us: gather_coupled(): pl.pallas_call(functools.partial(gather_kernel, n_pw, n_band), out_shape=...]
    dot_general x9 -> x0, matrix products: 11.1 us -> none  [the longest x1 2.78 us: shards(): jnp.einsum('pq,kqb->kpb', block, coeffs, precision=lax.Precision.HIGHEST)]
    all_gather x1 -> x0, blocking collectives: 10.5 us -> none  [shards(): gathered = lax.all_gather(projectors, 'band', axis=1, tiled=True)]
    another operation x1 -> x0, local copies, waits for them, and re-layouts: 7.27 us -> none  [spread_back(): return jnp.stack([real, imag])]
    unnamed x9 -> x5, local copies, waits for them, and re-layouts: 0.18 us -> 4.31 us
    another operation x2 -> x0, other arithmetic: 3.44 us -> none  [the longest x1 2.46 us: spread_back(): return jnp.stack([real, imag])]
  transfers between devices with their start and end apart: 1 -> 0, of which waited for: 1 -> 0; matrix products, arithmetic and copies ran while one was open for 1% -> 0% of each run, Pallas kernels for 0% -> 0%
where the time goes in v1:
time: 41.5 us; the launch traced here: 41.1 us
  Pallas kernels  33.8 us (81%)
  local copies, waits for them, and re-layouts  4.31 us (10%)
  matrix products  1.59 us (4%)
  other arithmetic  1.45 us (3%)
    pallas_call x1, Pallas kernels, gather_coupled(): pl.pallas_call(functools.partial(gather_kernel, n_pw, n_band), out_shape=...  29 us
    pallas_call x1, Pallas kernels, spread_back(): pl.pallas_call(spread_kernel, grid=(blocks,), out_shape=jax.ShapeDtypeStr...  4.73 us
    unnamed x5, local copies, waits for them, and re-layouts  4.31 us
    dot_general x2, matrix products, coupling_block(): jnp.einsum('api,aij,aqj->pq', select, sym, select, precision=lax.Precisio...  1.59 us

profile of v1, /device:TPU:1, one launch (start us, length us, event | category | flops | bytes accessed | tf_op | source)
XLA Modules:
  0.0 41.1 jit_solution(12655223167528863921)
XLA Ops:
  0.0 0.7 %iota_compare_fusion.1 = pred[12,13]{1,0:T(8,128)(4,1)S(1)} fusion(s32[12]{0:T(128)} %param.9), kind=kLoop, calls=%fused_computation.11 | loop fusion | flops 156 | bytes 204 | tf_op jit(solution)/shard_map/lt | solution.py:21
  0.7 0.7 %iota_add_fusion = s32[12,13]{1,0:T(8,128)S(1)} fusion(s32[12]{0:T(128)} %param.8), kind=kLoop, calls=%fused_computation.12 | loop fusion | flops 156 | bytes 672 | tf_op jit(solution)/shard_map/add | solution.py:19
  1.5 1.0 %copy.6 = f32[12,13,13]{1,2,0:T(8,128)S(1)} copy(f32[12,13,13]{2,1,0:T(8,128)} %param.7) | data formatting | bytes 16224 | tf_op args[2]
  2.5 1.2 %fusion.1 = f32[12,13,128]{2,1,0:T(8,128)S(1)} fusion(f32[12,13,13]{2,1,0:T(8,128)} %param.7, f32[12,13,13]{1,2,0:T(8,128)S(1)} %copy.6, s32[12,13]{1,0:T(8,128)S(1)} %iota_add_fusion, pred[12,13]{1,0:T(8,128)(4,1)S(1)} %iota_compare_fusion.1), kind=kOutput, calls=%fused_computation.3 | convolution fusion | flops 3159000 | bytes 96876 | tf_op jit(solution)/shard_map/api,aij,aqj->pq/dot_general | solution.py:25
  3.7 0.4 convolution_bitcast_fusion.block
  4.1 0.0 copy-start
  4.1 2.3 %copy-done = bf16[2,1280,896]{2,1,0:T(8,128)(2,1)S(1)} copy-done((bf16[2,1280,896]{2,1,0:T(8,128)(2,1)S(1)}, bf16[2,1280,896]{2,1,0:T(8,128)(2,1)}, u32[]{:S(2)}) %copy-start) | copy-done | bytes 4587544
  6.4 0.0 copy-start.1
  6.4 1.0 %copy-done.1 = bf16[2,64,1280]{2,1,0:T(8,128)(2,1)S(1)} copy-done((bf16[2,64,1280]{2,1,0:T(8,128)(2,1)S(1)}, bf16[2,64,1280]{2,1,0:T(8,128)(2,1)}, u32[]{:S(2)}) %copy-start.1) | copy-done | bytes 327704
  7.4 29.0 %gather_coupled.1 = (bf16[1280,256]{1,0:T(8,128)(2,1)S(1)}, bf16[2,7,128,128]{3,2,1,0:T(8,128)(2,1)S(1)}) custom-call(bf16[2,1280,896]{2,1,0:T(8,128)(2,1)S(1)} %copy-done, bf16[2,64,1280]{2,1,0:T(8,128)(2,1)S(1)} %copy-done.1, f32[128,128]{1,0:T(8,128)S(1)} %convolution_bitcast_fusion.block), custom_call_target="tpu_custom_call" | custom-call | tf_op jit(solution)/shard_map/gather_coupled/pallas_call | solution.py:218
  36.4 4.7 %spread_back.1 = bf16[2,1280,896]{2,1,0:T(8,128)(2,1)} custom-call(bf16[1280,256]{1,0:T(8,128)(2,1)S(1)} %get-tuple-element.7.pt, bf16[2,7,128,128]{3,2,1,0:T(8,128)(2,1)S(1)} %get-tuple-element.8.c), custom_call_target="tpu_custom_call" | custom-call | tf_op jit(solution)/shard_map/spread_back/pallas_call | solution.py:261
Async XLA Ops:
  4.1 2.3 %copy-start = (bf16[2,1280,896]{2,1,0:T(8,128)(2,1)S(1)}, bf16[2,1280,896]{2,1,0:T(8,128)(2,1)}, u32[]{:S(2)}) copy-start(bf16[2,1280,896]{2,1,0:T(8,128)(2,1)} %waves.1) | copy-start | bytes 13762564
  6.4 1.0 %copy-start.1 = (bf16[2,64,1280]{2,1,0:T(8,128)(2,1)S(1)}, bf16[2,64,1280]{2,1,0:T(8,128)(2,1)}, u32[]{:S(2)}) copy-start(bf16[2,64,1280]{2,1,0:T(8,128)(2,1)} %proj.1) | copy-start | bytes 983044

commit v2 on v1

v2 whole, which is shorter than its diff:
```python
import functools

import jax
import jax.numpy as jnp
from jax import lax
from jax.experimental import pallas as pl
from jax.experimental.pallas import tpu as pltpu
from jax.sharding import PartitionSpec as P

NP = 128
M = 13
LANES = 128
SLOT = 16
MESH = pl.DeviceIdType.MESH


def coupling_block(coupling, offsets, counts, spare):
    atoms, most, _ = coupling.shape
    wide = spare.shape[0]
    spare[...] = jnp.zeros_like(spare)
    for a in range(atoms):
        spare[a * SLOT:a * SLOT + most, :most] = coupling[a]

    def iota(shape, dim):
        return lax.broadcasted_iota(jnp.int32, shape, dim)

    place = iota((NP, wide), 1)
    atom, entry = lax.div(place, SLOT), lax.rem(place, SLOT)
    start = jnp.full((NP, wide), -wide, jnp.int32)
    count = jnp.zeros((NP, wide), jnp.int32)
    for a in range(atoms):
        start = jnp.where(atom == a, offsets[a], start)
        count = jnp.where(atom == a, counts[a], count)
    select = jnp.where((iota((NP, wide), 0) == start + entry) & (entry < count), 1.0, 0.0)
    repeat = jnp.where(lax.rem(iota((LANES, wide), 1), SLOT) == iota((LANES, wide), 0), 1.0, 0.0)
    same = lax.div(iota((wide, wide), 0), SLOT) == lax.div(iota((wide, wide), 1), SLOT)
    spread = dot_exact(spare[...], repeat, 0)
    spread = jnp.where(same, spread, 0.0)
    raw = dot_exact(dot_exact(select, spread, 0), select, 1)
    return (raw + raw.T) * 0.5


def dot_exact(a, b, dim):
    return lax.dot_general(a, b, (((1,), (dim,)), ((), ())), precision=lax.Precision.HIGHEST,
                           preferred_element_type=jnp.float32)


def column_tiles(columns):
    return [(start, min(256, columns - start)) for start in range(0, columns, 256)]


def windows_of(n_band, pieces, held, piece):
    if n_band != 2 or held < 2 * SLOT:
        return [None] * (pieces - 1) + [(0, NP)]
    ends = [held + i * piece - SLOT for i in range(pieces - 1)] + [NP]
    return [(first, end - first) for first, end in zip([0] + ends[:-1], ends)]


def gather_kernel(n_pw, n_band, waves, proj, coupling, offsets, counts, pt_out, c_out,
                  w, p_all, acc, sib, send, recv, total, c_all, pt, spare, block,
                  w_sem, own_sem, out_sem, p_send, p_recv, s_send, s_recv,
                  r_send, r_recv, g_send, g_recv, f_send, f_recv):
    pw = lax.axis_index("pw")
    band = lax.axis_index("band")
    chip, core = lax.div(pw, 2), lax.rem(pw, 2)
    chips = n_pw // 2
    held = proj.shape[1]
    columns = waves.shape[2]
    blocks = columns // LANES
    piece = min(32, held)
    subs = held // piece
    tiles = column_tiles(columns)
    sibling = (chip * 2 + 1 - core, band)
    windows = windows_of(n_band, 1 + (n_band - 1) * subs, held, piece)

    def chip_at(step):
        return lax.rem(chip + step, chips)

    def same_core(other):
        return (other * 2 + core, band)

    def sub_of(sender, s):
        return subs - 1 - s + sender * (2 * s - subs + 1) if n_band == 2 else s

    def window(i):
        first, size = windows[i]
        if first == 0 and size == NP:
            return pl.ds(0, NP)
        return pl.ds(pl.multiple_of(first + band * (NP - 2 * first - size), SLOT), size)

    own_rows = pl.multiple_of(band * held, held)
    own = pltpu.make_async_copy(proj, p_all.at[:, pl.ds(own_rows, held), :], own_sem.at[0])
    own.start()
    wave_copies = []
    for t, (start, size) in enumerate(tiles):
        copy = pltpu.make_async_copy(
            waves.at[:, :, pl.ds(start, size)], w.at[:, :, pl.ds(start, size)], w_sem.at[t])
        copy.start()
        wave_copies.append(copy)

    barrier = pltpu.get_barrier_semaphore()
    for d in range(1, n_band):
        pl.semaphore_signal(barrier, inc=1, device_id=(pw, lax.rem(band + d, n_band)), device_id_type=MESH)
    pl.semaphore_signal(barrier, inc=1, device_id=sibling, device_id_type=MESH)
    for d in range(1, chips):
        pl.semaphore_signal(barrier, inc=1, device_id=same_core(chip_at(d)), device_id_type=MESH)
    pl.semaphore_wait(barrier, n_band - 1 + 1 + chips - 1)

    p_copies = []
    for d in range(1, n_band):
        for s in range(subs):
            sub = sub_of(band, s)
            rows = pl.ds(pl.multiple_of(band * held + sub * piece, piece), piece)
            copy = pltpu.make_async_remote_copy(
                src_ref=proj.at[:, pl.ds(pl.multiple_of(sub * piece, piece), piece), :],
                dst_ref=p_all.at[:, rows, :],
                send_sem=p_send.at[d - 1, s], recv_sem=p_recv.at[d - 1, s],
                device_id=(pw, lax.rem(band + d, n_band)), device_id_type=MESH)
            copy.start()
            p_copies.append(copy)

    pieces = [(own_rows, held)]
    for d in range(1, n_band):
        source = lax.rem(band + n_band - d, n_band)
        for s in range(subs):
            row = pl.multiple_of(source * held + sub_of(source, s) * piece, piece)
            pieces.append((row, piece))
    last = len(pieces) - 1

    def project(i):
        row, size = pieces[i]
        rows = pl.ds(row, size)
        p0, p1 = p_all[0, rows, :], p_all[1, rows, :]
        lhs0 = jnp.concatenate([p0, -p1], axis=0)
        lhs1 = jnp.concatenate([p1, p0], axis=0)
        for t, (start, width) in enumerate(tiles):
            if i == 0:
                wave_copies[t].wait()
            cols = pl.ds(start, width)
            r = jnp.dot(lhs0, w[0, :, cols], preferred_element_type=jnp.float32)
            r += jnp.dot(lhs1, w[1, :, cols], preferred_element_type=jnp.float32)
            acc[0, rows, cols] = r[:size]
            acc[1, rows, cols] = r[size:]

    def sibling_copy(i):
        rows = pl.ds(*pieces[i])
        return pltpu.make_async_remote_copy(
            src_ref=acc.at[1 - core, rows, :], dst_ref=sib.at[rows, :],
            send_sem=s_send.at[i], recv_sem=s_recv.at[i],
            device_id=sibling, device_id_type=MESH)

    def reduce_copy(i, d):
        other = chip_at(d)
        rows = pl.ds(*pieces[i])
        return pltpu.make_async_remote_copy(
            src_ref=send.at[lax.min(other, blocks - 1), rows, :],
            dst_ref=recv.at[chip, rows, :],
            send_sem=r_send.at[i, d], recv_sem=r_recv.at[i, chip],
            device_id=same_core(other), device_id_type=MESH)

    def reduce_send(i):
        rows = pl.ds(*pieces[i])
        sibling_copy(i).wait_recv()
        for b in range(blocks):
            cols = pl.ds(b * LANES, LANES)
            send[b, rows, :] = (acc[core, rows, cols] + sib[rows, cols]).astype(jnp.bfloat16)
        for d in range(1, chips):
            pl.when(chip_at(d) < blocks)(lambda: reduce_copy(i, d).start())

    def gather_copy(i, b, d):
        rows = window(i)
        return pltpu.make_async_remote_copy(
            src_ref=c_all.at[core, b, rows, :], dst_ref=c_all.at[core, b, rows, :],
            send_sem=g_send.at[i, d], recv_sem=g_recv.at[i, b],
            device_id=same_core(chip_at(d)), device_id_type=MESH)

    def forward_copy(i, k, b):
        rows = window(i)
        return pltpu.make_async_remote_copy(
            src_ref=c_all.at[k, b, rows, :], dst_ref=c_all.at[k, b, rows, :],
            send_sem=f_send.at[i, b], recv_sem=f_recv.at[i, b],
            device_id=sibling, device_id_type=MESH)

    def couple(i):
        rows = pl.ds(*pieces[i])

        @pl.when(chip < blocks)
        def _():
            value = send[chip, rows, :].astype(jnp.float32)
            for d in range(1, chips):
                source = chip_at(d)
                pltpu.make_async_remote_copy(
                    src_ref=send.at[0, rows, :], dst_ref=recv.at[source, rows, :],
                    send_sem=r_send.at[i, d], recv_sem=r_recv.at[i, source],
                    device_id=same_core(source), device_id_type=MESH).wait_recv()
                value += recv[source, rows, :].astype(jnp.float32)
            total[rows, :] = value
            if windows[i] is not None:
                c_all[core, chip, window(i), :] = dot_exact(
                    block[window(i), :], total[...], 0).astype(jnp.bfloat16)
                for d in range(1, chips):
                    gather_copy(i, chip, d).start()
                forward_copy(i, core, chip).start()

    def forward(i):
        if windows[i] is None:
            return
        for d in range(1, chips):
            source = chip_at(d)

            @pl.when(source < blocks)
            def _():
                gather_copy(i, source, d).wait_recv()
                forward_copy(i, core, source).start()

    total[...] = jnp.zeros_like(total)
    own.wait()
    project(0)
    sibling_copy(0).start()
    block[...] = coupling_block(coupling, offsets, counts, spare)
    reduce_send(0)
    for i in range(1, last + 1):
        p_copies[i - 1].wait_recv()
        project(i)
        sibling_copy(i).start()
        couple(i - 1)
        reduce_send(i)
        if i >= 2:
            forward(i - 2)

    pt[:, :NP] = p_all[0].T
    pt[:, NP:] = p_all[1].T
    pt_copy = pltpu.make_async_copy(pt, pt_out, out_sem.at[0])
    pt_copy.start()
    couple(last)
    if last >= 1:
        forward(last - 1)
    forward(last)

    wanted = [i for i in range(last + 1) if windows[i] is not None]
    for i in wanted:
        for b in range(blocks):
            forward_copy(i, 1 - core, b).wait_recv()
    c_copy = pltpu.make_async_copy(c_all, c_out, out_sem.at[1])
    c_copy.start()

    for copy in p_copies:
        copy.wait_send()
    for i in range(last + 1):
        sibling_copy(i).wait_send()
        for d in range(1, chips):
            pl.when(chip_at(d) < blocks)(lambda: reduce_copy(i, d).wait_send())

    @pl.when(chip < blocks)
    def _():
        for i in wanted:
            for d in range(1, chips):
                gather_copy(i, chip, d).wait_send()
    for i in wanted:
        for b in range(blocks):
            forward_copy(i, core, b).wait_send()
    pt_copy.wait()
    c_copy.wait()


def gather_coupled(n_pw, n_band, waves, projectors, coupling, offsets, counts):
    _, depth, columns = waves.shape
    held = projectors.shape[1]
    chips = n_pw // 2
    blocks = columns // LANES
    subs = held // min(32, held)
    pieces = 1 + (n_band - 1) * subs
    bf16, f32 = jnp.bfloat16, jnp.float32
    dma = pltpu.SemaphoreType.DMA
    hbm = pl.BlockSpec(memory_space=pltpu.HBM)
    anywhere = pl.BlockSpec(memory_space=pl.ANY)
    scalars = pl.BlockSpec(memory_space=pltpu.SMEM)
    wide = -(-coupling.shape[0] * SLOT // LANES) * LANES
    return pl.pallas_call(
        functools.partial(gather_kernel, n_pw, n_band),
        out_shape=[
            jax.ShapeDtypeStruct((depth, 2 * NP), bf16),
            jax.ShapeDtypeStruct((2, blocks, NP, LANES), bf16),
        ],
        in_specs=[hbm, hbm, pl.BlockSpec(memory_space=pltpu.VMEM), scalars, scalars],
        out_specs=[anywhere, anywhere],
        scratch_shapes=[
            pltpu.VMEM((2, depth, columns), bf16),
            pltpu.VMEM((2, NP, depth), bf16),
            pltpu.VMEM((2, NP, columns), f32),
            pltpu.VMEM((NP, columns), f32),
            pltpu.VMEM((blocks, NP, LANES), bf16),
            pltpu.VMEM((chips, NP, LANES), bf16),
            pltpu.VMEM((NP, LANES), f32),
            pltpu.VMEM((2, blocks, NP, LANES), bf16),
            pltpu.VMEM((depth, 2 * NP), bf16),
            pltpu.VMEM((wide, LANES), f32),
            pltpu.VMEM((NP, NP), f32),
            dma((len(column_tiles(columns)),)), dma((1,)), dma((2,)),
            dma((n_band - 1, subs)), dma((n_band - 1, subs)),
            dma((pieces,)), dma((pieces,)),
            dma((pieces, chips)), dma((pieces, chips)),
            dma((pieces, chips)), dma((pieces, blocks)),
            dma((pieces, blocks)), dma((pieces, blocks)),
        ],
        compiler_params=pltpu.CompilerParams(
            collective_id=0, has_side_effects=True, vmem_limit_bytes=60 * 2**20),
        name="gather_coupled",
    )(waves, projectors, coupling, offsets, counts)


def spread_kernel(pt, c, out, rhs):
    blocks = c.shape[1]

    @pl.when(pl.program_id(0) == 0)
    def _():
        for b in range(blocks):
            c0, c1 = c[0, b], c[1, b]
            rhs[b, :NP, :LANES] = c0
            rhs[b, :NP, LANES:] = c1
            rhs[b, NP:, :LANES] = -c1
            rhs[b, NP:, LANES:] = c0

    for b in range(blocks):
        r = jnp.dot(pt[...], rhs[b], preferred_element_type=jnp.float32)
        out[0, :, b * LANES:(b + 1) * LANES] = r[:, :LANES].astype(out.dtype)
        out[1, :, b * LANES:(b + 1) * LANES] = r[:, LANES:].astype(out.dtype)


def spread_back(pt, coupled):
    depth = pt.shape[0]
    blocks = coupled.shape[1]
    rows = 256 if depth % 256 == 0 else depth
    return pl.pallas_call(
        spread_kernel,
        grid=(depth // rows,),
        out_shape=jax.ShapeDtypeStruct((2, depth, blocks * LANES), jnp.bfloat16),
        in_specs=[
            pl.BlockSpec((rows, 2 * NP), lambda r: (r, 0)),
            pl.BlockSpec((2, blocks, NP, LANES), lambda r: (0, 0, 0, 0)),
        ],
        out_specs=pl.BlockSpec((2, rows, blocks * LANES), lambda r: (0, r, 0)),
        scratch_shapes=[pltpu.VMEM((blocks, 2 * NP, 2 * LANES), jnp.bfloat16)],
        compiler_params=pltpu.CompilerParams(vmem_limit_bytes=60 * 2**20),
        name="spread_back",
    )(pt, coupled)


def solution(mesh):
    n_pw, n_band = mesh.shape["pw"], mesh.shape["band"]

    def shards(waves, projectors, coupling, offsets, counts):
        pt, coupled = gather_coupled(n_pw, n_band, waves, projectors, coupling, offsets, counts)
        return spread_back(pt, coupled)

    placed = (P(None, "pw", "band"), P(None, "band", "pw"), P(), P(), P())
    return jax.shard_map(
        shards, mesh=mesh, in_specs=placed, out_specs=P(None, "pw", "band"), check_vma=False
    )
```

time: 41.5 us -> 38.3 us (0.923)
  local copies, waits for them, and re-layouts: 4.31 us -> 0 us
  Pallas kernels: 33.8 us -> 38 us
  matrix products: 1.59 us -> 0 us
  other arithmetic: 1.45 us -> 0 us
    unnamed x5 -> x0, local copies, waits for them, and re-layouts: 4.31 us -> none
    pallas_call x1, Pallas kernels: 29 us -> 32.4 us  [gather_coupled(): pl.pallas_call(functools.partial(gather_kernel, n_pw, n_band), out_shape=...]
    dot_general x2 -> x0, matrix products: 1.59 us -> none  [coupling_block(): jnp.einsum('api,aij,aqj->pq', select, sym, select, precision=lax.Precisio...]
    pallas_call x1, Pallas kernels: 4.73 us -> 5.59 us  [spread_back(): pl.pallas_call(spread_kernel, grid=(depth // rows,), out_shape=jax.ShapeD...]
    lt x1 -> x0, other arithmetic: 0.73 us -> none  [coupling_block(): local[None, None, :] < counts[:, None, None]]
    add x1 -> x0, other arithmetic: 0.73 us -> none  [coupling_block(): target = offsets[:, None] + local[None, :]]
where the time goes in v2:
time: 38.3 us; the launch traced here: 38 us
  Pallas kernels  38 us (99%)
    pallas_call x1, Pallas kernels, gather_coupled(): pl.pallas_call(functools.partial(gather_kernel, n_pw, n_band), out_shape=...  32.4 us
    pallas_call x1, Pallas kernels, spread_back(): pl.pallas_call(spread_kernel, grid=(depth // rows,), out_shape=jax.ShapeD...  5.59 us

profile of v2, /device:TPU:1, one launch (start us, length us, event | category | flops | bytes accessed | tf_op | source)
XLA Modules:
  0.0 38.0 jit_solution(16021230048943705874)
XLA Ops:
  0.0 32.4 %gather_coupled.1 = (bf16[1280,256]{1,0:T(8,128)(2,1)}, bf16[2,7,128,128]{3,2,1,0:T(8,128)(2,1)}) custom-call(bf16[2,1280,896]{2,1,0:T(8,128)(2,1)} %waves.1, bf16[2,64,1280]{2,1,0:T(8,128)(2,1)} %proj.1, f32[12,13,13]{2,1,0:T(8,128)} %coupling.1, s32[12]{0:T(128)} %offsets.1, s32[12]{0:T(128)} %counts.1), custom_call_target="tpu_custom_call" | custom-call | tf_op jit(solution)/shard_map/gather_coupled/pallas_call | solution.py:279
  32.4 5.6 %spread_back.1 = bf16[2,1280,896]{2,1,0:T(8,128)(2,1)} custom-call(bf16[1280,256]{1,0:T(8,128)(2,1)} %get-tuple-element.7.pt, bf16[2,7,128,128]{3,2,1,0:T(8,128)(2,1)} %get-tuple-element.8.c), custom_call_target="tpu_custom_call" | custom-call | tf_op jit(solution)/shard_map/spread_back/pallas_call | solution.py:334

commit v3 on v2

--- a/solution.py
+++ b/solution.py
@@ -49,17 +49,23 @@
     return [(start, min(256, columns - start)) for start in range(0, columns, 256)]
 
 
-def windows_of(n_band, pieces, held, piece):
-    if n_band != 2 or held < 2 * SLOT:
-        return [None] * (pieces - 1) + [(0, NP)]
-    ends = [held + i * piece - SLOT for i in range(pieces - 1)] + [NP]
+def pieces_of(n_band, held):
+    return [held - SLOT, SLOT] if n_band == 2 and held > SLOT else [held]
+
+
+def windows_of(n_band, held):
+    sizes = pieces_of(n_band, held)
+    if n_band != 2 or held <= SLOT:
+        return [None] * ((n_band - 1) * len(sizes)) + [(0, NP)]
+    ends = [held - SLOT] + [held + sum(sizes[:s + 1]) - SLOT for s in range(len(sizes))]
+    ends[-1] = NP
     return [(first, end - first) for first, end in zip([0] + ends[:-1], ends)]
 
 
 def gather_kernel(n_pw, n_band, waves, proj, coupling, offsets, counts, pt_out, c_out,
-                  w, p_all, acc, sib, send, recv, total, c_all, pt, spare, block,
+                  w, p_all, acc, sib, send, recv, last_send, last_recv, total, c_all, pt, spare, block,
                   w_sem, own_sem, out_sem, p_send, p_recv, s_send, s_recv,
-                  r_send, r_recv, g_send, g_recv, f_send, f_recv):
+                  r_send, r_recv, l_send, l_recv, g_send, g_recv, f_send, f_recv, h_send, h_recv):
     pw = lax.axis_index("pw")
     band = lax.axis_index("band")
     chip, core = lax.div(pw, 2), lax.rem(pw, 2)
@@ -67,20 +73,26 @@
     held = proj.shape[1]
     columns = waves.shape[2]
     blocks = columns // LANES
-    piece = min(32, held)
-    subs = held // piece
+    sizes = pieces_of(n_band, held)
     tiles = column_tiles(columns)
     sibling = (chip * 2 + 1 - core, band)
-    windows = windows_of(n_band, 1 + (n_band - 1) * subs, held, piece)
+    windows = windows_of(n_band, held)
+    bf16 = jnp.bfloat16
 
     def chip_at(step):
         return lax.rem(chip + step, chips)
 
+    def pw_at(step):
+        return lax.rem(pw + step, n_pw)
+
     def same_core(other):
         return (other * 2 + core, band)
 
-    def sub_of(sender, s):
-        return subs - 1 - s + sender * (2 * s - subs + 1) if n_band == 2 else s
+    def sub_row(sender, s):
+        if n_band != 2:
+            return 0
+        first = sum(sizes[:s])
+        return pl.multiple_of(first + (1 - sender) * (held - 2 * first - sizes[s]), SLOT)
 
     def window(i):
         first, size = windows[i]
@@ -99,21 +111,19 @@
         wave_copies.append(copy)
 
     barrier = pltpu.get_barrier_semaphore()
+    for d in range(1, n_pw):
+        pl.semaphore_signal(barrier, inc=1, device_id=(pw_at(d), band), device_id_type=MESH)
     for d in range(1, n_band):
         pl.semaphore_signal(barrier, inc=1, device_id=(pw, lax.rem(band + d, n_band)), device_id_type=MESH)
-    pl.semaphore_signal(barrier, inc=1, device_id=sibling, device_id_type=MESH)
-    for d in range(1, chips):
-        pl.semaphore_signal(barrier, inc=1, device_id=same_core(chip_at(d)), device_id_type=MESH)
-    pl.semaphore_wait(barrier, n_band - 1 + 1 + chips - 1)
+    pl.semaphore_wait(barrier, n_band - 1 + n_pw - 1)
 
     p_copies = []
     for d in range(1, n_band):
-        for s in range(subs):
-            sub = sub_of(band, s)
-            rows = pl.ds(pl.multiple_of(band * held + sub * piece, piece), piece)
+        for s, size in enumerate(sizes):
+            row = sub_row(band, s)
             copy = pltpu.make_async_remote_copy(
-                src_ref=proj.at[:, pl.ds(pl.multiple_of(sub * piece, piece), piece), :],
-                dst_ref=p_all.at[:, rows, :],
+                src_ref=proj.at[:, pl.ds(row, size), :],
+                dst_ref=p_all.at[:, pl.ds(pl.multiple_of(own_rows + row, SLOT), size), :],
                 send_sem=p_send.at[d - 1, s], recv_sem=p_recv.at[d - 1, s],
                 device_id=(pw, lax.rem(band + d, n_band)), device_id_type=MESH)
             copy.start()
@@ -122,9 +132,8 @@
     pieces = [(own_rows, held)]
     for d in range(1, n_band):
         source = lax.rem(band + n_band - d, n_band)
-        for s in range(subs):
-            row = pl.multiple_of(source * held + sub_of(source, s) * piece, piece)
-            pieces.append((row, piece))
+        for s, size in enumerate(sizes):
+            pieces.append((pl.multiple_of(source * held + sub_row(source, s), SLOT), size))
     last = len(pieces) - 1
 
     def project(i):
@@ -139,8 +148,13 @@
             cols = pl.ds(start, width)
             r = jnp.dot(lhs0, w[0, :, cols], preferred_element_type=jnp.float32)
             r += jnp.dot(lhs1, w[1, :, cols], preferred_element_type=jnp.float32)
-            acc[0, rows, cols] = r[:size]
-            acc[1, rows, cols] = r[size:]
+            if i == last:
+                for c in range(0, width, LANES):
+                    last_send[0, (start + c) // LANES] = r[:size, c:c + LANES].astype(bf16)
+                    last_send[1, (start + c) // LANES] = r[size:, c:c + LANES].astype(bf16)
+            else:
+                acc[0, rows, cols] = r[:size]
+                acc[1, rows, cols] = r[size:]
 
     def sibling_copy(i):
         rows = pl.ds(*pieces[i])
@@ -163,9 +177,17 @@
         sibling_copy(i).wait_recv()
         for b in range(blocks):
             cols = pl.ds(b * LANES, LANES)
-            send[b, rows, :] = (acc[core, rows, cols] + sib[rows, cols]).astype(jnp.bfloat16)
+            send[b, rows, :] = (acc[core, rows, cols] + sib[rows, cols]).astype(bf16)
         for d in range(1, chips):
             pl.when(chip_at(d) < blocks)(lambda: reduce_copy(i, d).start())
+
+    def last_copy(e):
+        target = pw_at(e)
+        return pltpu.make_async_remote_copy(
+            src_ref=last_send.at[lax.rem(target, 2), lax.min(lax.div(target, 2), blocks - 1)],
+            dst_ref=last_recv.at[pw],
+            send_sem=l_send.at[e], recv_sem=l_recv.at[pw],
+            device_id=(target, band), device_id_type=MESH)
 
     def gather_copy(i, b, d):
         rows = window(i)
@@ -181,11 +203,24 @@
             send_sem=f_send.at[i, b], recv_sem=f_recv.at[i, b],
             device_id=sibling, device_id_type=MESH)
 
+    def final_copy(owner, e):
+        here = c_all.at[lax.rem(owner, 2), lax.min(lax.div(owner, 2), blocks - 1), window(last), :]
+        return pltpu.make_async_remote_copy(
+            src_ref=here, dst_ref=here, send_sem=h_send.at[e], recv_sem=h_recv.at[owner],
+            device_id=(pw_at(e), band), device_id_type=MESH)
+
     def couple(i):
         rows = pl.ds(*pieces[i])
-
-        @pl.when(chip < blocks)
-        def _():
+        if i == last:
+            value = last_send[core, chip].astype(jnp.float32)
+            for e in range(1, n_pw):
+                source = pw_at(e)
+                pltpu.make_async_remote_copy(
+                    src_ref=last_send.at[0, 0], dst_ref=last_recv.at[source],
+                    send_sem=l_send.at[e], recv_sem=l_recv.at[source],
+                    device_id=(source, band), device_id_type=MESH).wait_recv()
+                value += last_recv[source].astype(jnp.float32)
+        else:
             value = send[chip, rows, :].astype(jnp.float32)
             for d in range(1, chips):
                 source = chip_at(d)
@@ -194,17 +229,19 @@
                     send_sem=r_send.at[i, d], recv_sem=r_recv.at[i, source],
                     device_id=same_core(source), device_id_type=MESH).wait_recv()
                 value += recv[source, rows, :].astype(jnp.float32)
-            total[rows, :] = value
-            if windows[i] is not None:
-                c_all[core, chip, window(i), :] = dot_exact(
-                    block[window(i), :], total[...], 0).astype(jnp.bfloat16)
-                for d in range(1, chips):
-                    gather_copy(i, chip, d).start()
-                forward_copy(i, core, chip).start()
-
-    def forward(i):
+        total[rows, :] = value
         if windows[i] is None:
             return
+        c_all[core, chip, window(i), :] = dot_exact(block[window(i), :], total[...], 0).astype(bf16)
+        if i == last:
+            for e in range(1, n_pw):
+                final_copy(pw, e).start()
+        else:
+            for d in range(1, chips):
+                gather_copy(i, chip, d).start()
+            forward_copy(i, core, chip).start()
+
+    def forward(i):
         for d in range(1, chips):
             source = chip_at(d)
 
@@ -213,54 +250,71 @@
                 gather_copy(i, source, d).wait_recv()
                 forward_copy(i, core, source).start()
 
-    total[...] = jnp.zeros_like(total)
+    def out_copy(i):
+        rows = window(i)
+        return pltpu.make_async_copy(
+            c_all.at[:, :, rows, :], c_out.at[:, :, rows, :], out_sem.at[i + 1])
+
+    early = [i for i in range(last) if windows[i] is not None]
+    owns = chip < blocks
+
     own.wait()
     project(0)
-    sibling_copy(0).start()
+    if last > 0:
+        sibling_copy(0).start()
+        total[...] = jnp.zeros_like(total)
+        reduce_send(0)
     block[...] = coupling_block(coupling, offsets, counts, spare)
-    reduce_send(0)
     for i in range(1, last + 1):
         p_copies[i - 1].wait_recv()
         project(i)
-        sibling_copy(i).start()
-        couple(i - 1)
-        reduce_send(i)
-        if i >= 2:
-            forward(i - 2)
+        if i < last:
+            sibling_copy(i).start()
+            reduce_send(i)
+    for e in range(1, n_pw):
+        pl.when(lax.div(pw_at(e), 2) < blocks)(lambda: last_copy(e).start())
+
+    for i in range(last):
+        pl.when(owns)(lambda: couple(i))
 
     pt[:, :NP] = p_all[0].T
     pt[:, NP:] = p_all[1].T
     pt_copy = pltpu.make_async_copy(pt, pt_out, out_sem.at[0])
     pt_copy.start()
-    couple(last)
-    if last >= 1:
-        forward(last - 1)
-    forward(last)
-
-    wanted = [i for i in range(last + 1) if windows[i] is not None]
-    for i in wanted:
-        for b in range(blocks):
-            forward_copy(i, 1 - core, b).wait_recv()
-    c_copy = pltpu.make_async_copy(c_all, c_out, out_sem.at[1])
-    c_copy.start()
-
     for copy in p_copies:
         copy.wait_send()
-    for i in range(last + 1):
+    for i in range(last):
         sibling_copy(i).wait_send()
         for d in range(1, chips):
             pl.when(chip_at(d) < blocks)(lambda: reduce_copy(i, d).wait_send())
 
-    @pl.when(chip < blocks)
+    pl.when(owns)(lambda: couple(last))
+    for i in early:
+        forward(i)
+    for i in early:
+        for b in range(blocks):
+            forward_copy(i, 1 - core, b).wait_recv()
+        out_copy(i).start()
+    for e in range(1, n_pw):
+        pl.when(lax.div(pw_at(e), 2) < blocks)(lambda: final_copy(pw_at(e), e).wait_recv())
+    out_copy(last).start()
+
+    for e in range(1, n_pw):
+        pl.when(lax.div(pw_at(e), 2) < blocks)(lambda: last_copy(e).wait_send())
+
+    @pl.when(owns)
     def _():
-        for i in wanted:
+        for i in early:
             for d in range(1, chips):
                 gather_copy(i, chip, d).wait_send()
-    for i in wanted:
+        for e in range(1, n_pw):
+            final_copy(pw, e).wait_send()
+    for i in early:
         for b in range(blocks):
             forward_copy(i, core, b).wait_send()
+        out_copy(i).wait()
     pt_copy.wait()
-    c_copy.wait()
+    out_copy(last).wait()
 
 
 def gather_coupled(n_pw, n_band, waves, projectors, coupling, offsets, counts):
@@ -268,8 +322,10 @@
     held = projectors.shape[1]
     chips = n_pw // 2
     blocks = columns // LANES
-    subs = held // min(32, held)
+    sizes = pieces_of(n_band, held)
+    subs = len(sizes)
     pieces = 1 + (n_band - 1) * subs
+    last_rows = sizes[-1]
     bf16, f32 = jnp.bfloat16, jnp.float32
     dma = pltpu.SemaphoreType.DMA
     hbm = pl.BlockSpec(memory_space=pltpu.HBM)
@@ -291,17 +347,21 @@
             pltpu.VMEM((NP, columns), f32),
             pltpu.VMEM((blocks, NP, LANES), bf16),
             pltpu.VMEM((chips, NP, LANES), bf16),
+            pltpu.VMEM((2, blocks, last_rows, LANES), bf16),
+            pltpu.VMEM((n_pw, last_rows, LANES), bf16),
             pltpu.VMEM((NP, LANES), f32),
             pltpu.VMEM((2, blocks, NP, LANES), bf16),
             pltpu.VMEM((depth, 2 * NP), bf16),
             pltpu.VMEM((wide, LANES), f32),
             pltpu.VMEM((NP, NP), f32),
-            dma((len(column_tiles(columns)),)), dma((1,)), dma((2,)),
+            dma((len(column_tiles(columns)),)), dma((1,)), dma((1 + pieces,)),
             dma((n_band - 1, subs)), dma((n_band - 1, subs)),
             dma((pieces,)), dma((pieces,)),
             dma((pieces, chips)), dma((pieces, chips)),
+            dma((n_pw,)), dma((n_pw,)),
             dma((pieces, chips)), dma((pieces, blocks)),
             dma((pieces, blocks)), dma((pieces, blocks)),
+            dma((n_pw,)), dma((n_pw,)),
         ],
         compiler_params=pltpu.CompilerParams(
             collective_id=0, has_side_effects=True, vmem_limit_bytes=60 * 2**20),
@@ -309,38 +369,66 @@
     )(waves, projectors, coupling, offsets, counts)
 
 
-def spread_kernel(pt, c, out, rhs):
+def row_parts(depth):
+    ends = list(range(512, depth, 512)) + [depth]
+    return [(first, end - first) for first, end in zip([0] + ends[:-1], ends)]
+
+
+def spread_kernel(pt, c, out, pt_vmem, c_vmem, rhs, result, in_sem, out_sem):
     blocks = c.shape[1]
-
-    @pl.when(pl.program_id(0) == 0)
-    def _():
+    parts = row_parts(pt.shape[0])
+    c_copy = pltpu.make_async_copy(c, c_vmem, in_sem.at[0])
+    c_copy.start()
+    pt_copies = []
+    for i, (first, size) in enumerate(parts):
+        rows = pl.ds(first, size)
+        copy = pltpu.make_async_copy(pt.at[rows, :], pt_vmem.at[rows, :], in_sem.at[i + 1])
+        copy.start()
+        pt_copies.append(copy)
+    c_copy.wait()
+    for b in range(blocks):
+        c0, c1 = c_vmem[0, b], c_vmem[1, b]
+        rhs[b, :NP, :LANES] = c0
+        rhs[b, :NP, LANES:] = c1
+        rhs[b, NP:, :LANES] = -c1
+        rhs[b, NP:, LANES:] = c0
+    out_copies = []
+    for i, (first, size) in enumerate(parts):
+        rows = pl.ds(first, size)
+        pt_copies[i].wait()
         for b in range(blocks):
-            c0, c1 = c[0, b], c[1, b]
-            rhs[b, :NP, :LANES] = c0
-            rhs[b, :NP, LANES:] = c1
-            rhs[b, NP:, :LANES] = -c1
-            rhs[b, NP:, LANES:] = c0
-
-    for b in range(blocks):
-        r = jnp.dot(pt[...], rhs[b], preferred_element_type=jnp.float32)
-        out[0, :, b * LANES:(b + 1) * LANES] = r[:, :LANES].astype(out.dtype)
-        out[1, :, b * LANES:(b + 1) * LANES] = r[:, LANES:].astype(out.dtype)
+            cols = pl.ds(b * LANES, LANES)
+            r = jnp.dot(pt_vmem[rows, :], rhs[b], preferred_element_type=jnp.float32)
+            result[0, rows, cols] = r[:, :LANES].astype(result.dtype)
+            result[1, rows, cols] = r[:, LANES:].astype(result.dtype)
+        for k in range(2):
+            copy = pltpu.make_async_copy(
+                result.at[k, rows, :], out.at[k, rows, :], out_sem.at[i, k])
+            copy.start()
+            out_copies.append(copy)
+    for copy in out_copies:
+        copy.wait()
 
 
 def spread_back(pt, coupled):
     depth = pt.shape[0]
     blocks = coupled.shape[1]
-    rows = 256 if depth % 256 == 0 else depth
+    parts = len(row_parts(depth))
+    bf16 = jnp.bfloat16
+    anywhere = pl.BlockSpec(memory_space=pl.ANY)
     return pl.pallas_call(
         spread_kernel,
-        grid=(depth // rows,),
-        out_shape=jax.ShapeDtypeStruct((2, depth, blocks * LANES), jnp.bfloat16),
-        in_specs=[
-            pl.BlockSpec((rows, 2 * NP), lambda r: (r, 0)),
-            pl.BlockSpec((2, blocks, NP, LANES), lambda r: (0, 0, 0, 0)),
+        out_shape=jax.ShapeDtypeStruct((2, depth, blocks * LANES), bf16),
+        in_specs=[anywhere, anywhere],
+        out_specs=anywhere,
+        scratch_shapes=[
+            pltpu.VMEM(pt.shape, bf16),
+            pltpu.VMEM(coupled.shape, bf16),
+            pltpu.VMEM((blocks, 2 * NP, 2 * LANES), bf16),
+            pltpu.VMEM((2, depth, blocks * LANES), bf16),
+            pltpu.SemaphoreType.DMA((1 + parts,)),
+            pltpu.SemaphoreType.DMA((parts, 2)),
         ],
-        out_specs=pl.BlockSpec((2, rows, blocks * LANES), lambda r: (0, r, 0)),
-        scratch_shapes=[pltpu.VMEM((blocks, 2 * NP, 2 * LANES), jnp.bfloat16)],
         compiler_params=pltpu.CompilerParams(vmem_limit_bytes=60 * 2**20),
         name="spread_back",
     )(pt, coupled)

time: 38.3 us -> 34.9 us (0.911)
  Pallas kernels: 38 us -> 34.4 us
    pallas_call x1, Pallas kernels: 32.4 us -> 30.3 us  [gather_coupled(): pl.pallas_call(functools.partial(gather_kernel, n_pw, n_band), out_shape=...]
    pallas_call x1, Pallas kernels: 5.59 us -> 4.14 us  [spread_back(): pl.pallas_call(spread_kernel, out_shape=jax.ShapeDtypeStruct((2, depth, b...]
where the time goes in v3:
time: 34.9 us; the launch traced here: 34.5 us
  Pallas kernels  34.4 us (99%)
    pallas_call x1, Pallas kernels, gather_coupled(): pl.pallas_call(functools.partial(gather_kernel, n_pw, n_band), out_shape=...  30.3 us
    pallas_call x1, Pallas kernels, spread_back(): pl.pallas_call(spread_kernel, out_shape=jax.ShapeDtypeStruct((2, depth, b...  4.14 us

profile of v3, /device:TPU:1, one launch (start us, length us, event | category | flops | bytes accessed | tf_op | source)
XLA Modules:
  0.0 34.5 jit_solution(6895214585316783234)
XLA Ops:
  0.0 30.3 %gather_coupled.1 = (bf16[1280,256]{1,0:T(8,128)(2,1)}, bf16[2,7,128,128]{3,2,1,0:T(8,128)(2,1)}) custom-call(bf16[2,1280,896]{2,1,0:T(8,128)(2,1)} %waves.1, bf16[2,64,1280]{2,1,0:T(8,128)(2,1)} %proj.1, f32[12,13,13]{2,1,0:T(8,128)} %coupling.1, s32[12]{0:T(128)} %offsets.1, s32[12]{0:T(128)} %counts.1), custom_call_target="tpu_custom_call" | custom-call | tf_op jit(solution)/shard_map/gather_coupled/pallas_call | solution.py:335
  30.3 4.1 %spread_back.1 = bf16[2,1280,896]{2,1,0:T(8,128)(2,1)} custom-call(bf16[1280,256]{1,0:T(8,128)(2,1)} %get-tuple-element.7.pt, bf16[2,7,128,128]{3,2,1,0:T(8,128)(2,1)} %get-tuple-element.8.c), custom_call_target="tpu_custom_call" | custom-call | tf_op jit(solution)/shard_map/spread_back/pallas_call | solution.py:419

commit v4 on v3

--- a/solution.py
+++ b/solution.py
@@ -57,9 +57,8 @@
     sizes = pieces_of(n_band, held)
     if n_band != 2 or held <= SLOT:
         return [None] * ((n_band - 1) * len(sizes)) + [(0, NP)]
-    ends = [held - SLOT] + [held + sum(sizes[:s + 1]) - SLOT for s in range(len(sizes))]
-    ends[-1] = NP
-    return [(first, end - first) for first, end in zip([0] + ends[:-1], ends)]
+    early = NP - sizes[-1] - SLOT
+    return [None] * (len(sizes) - 1) + [(0, early), (early, NP - early)]
 
 
 def gather_kernel(n_pw, n_band, waves, proj, coupling, offsets, counts, pt_out, c_out,
@@ -274,31 +273,26 @@
     for e in range(1, n_pw):
         pl.when(lax.div(pw_at(e), 2) < blocks)(lambda: last_copy(e).start())
 
-    for i in range(last):
+    for i in range(last + 1):
         pl.when(owns)(lambda: couple(i))
+    for i in early:
+        forward(i)
 
     pt[:, :NP] = p_all[0].T
     pt[:, NP:] = p_all[1].T
     pt_copy = pltpu.make_async_copy(pt, pt_out, out_sem.at[0])
     pt_copy.start()
+    for i in early:
+        for b in range(blocks):
+            forward_copy(i, 1 - core, b).wait_recv()
+        out_copy(i).start()
+
     for copy in p_copies:
         copy.wait_send()
     for i in range(last):
         sibling_copy(i).wait_send()
         for d in range(1, chips):
             pl.when(chip_at(d) < blocks)(lambda: reduce_copy(i, d).wait_send())
-
-    pl.when(owns)(lambda: couple(last))
-    for i in early:
-        forward(i)
-    for i in early:
-        for b in range(blocks):
-            forward_copy(i, 1 - core, b).wait_recv()
-        out_copy(i).start()
-    for e in range(1, n_pw):
-        pl.when(lax.div(pw_at(e), 2) < blocks)(lambda: final_copy(pw_at(e), e).wait_recv())
-    out_copy(last).start()
-
     for e in range(1, n_pw):
         pl.when(lax.div(pw_at(e), 2) < blocks)(lambda: last_copy(e).wait_send())
 
@@ -312,8 +306,13 @@
     for i in early:
         for b in range(blocks):
             forward_copy(i, core, b).wait_send()
+
+    for e in range(1, n_pw):
+        pl.when(lax.div(pw_at(e), 2) < blocks)(lambda: final_copy(pw_at(e), e).wait_recv())
+    out_copy(last).start()
+    pt_copy.wait()
+    for i in early:
         out_copy(i).wait()
-    pt_copy.wait()
     out_copy(last).wait()
 
 
@@ -370,7 +369,7 @@
 
 
 def row_parts(depth):
-    ends = list(range(512, depth, 512)) + [depth]
+    ends = [end for end in (128, 512, 1024) if end < depth] + [depth]
     return [(first, end - first) for first, end in zip([0] + ends[:-1], ends)]
 
 

time: 34.9 us -> 35.6 us (1.020)
  Pallas kernels: 34.4 us -> 35.3 us
    pallas_call x1, Pallas kernels: 30.3 us -> 30.9 us  [gather_coupled(): pl.pallas_call(functools.partial(gather_kernel, n_pw, n_band), out_shape=...]
where the time goes in v4:
time: 35.6 us; the launch traced here: 35.3 us
  Pallas kernels  35.3 us (99%)
    pallas_call x1, Pallas kernels, gather_coupled(): pl.pallas_call(functools.partial(gather_kernel, n_pw, n_band), out_shape=...  30.9 us
    pallas_call x1, Pallas kernels, spread_back(): pl.pallas_call(spread_kernel, out_shape=jax.ShapeDtypeStruct((2, depth, b...  4.37 us

profile of v4, /device:TPU:1, one launch (start us, length us, event | category | flops | bytes accessed | tf_op | source)
XLA Modules:
  0.0 35.3 jit_solution(591028134840648194)
XLA Ops:
  0.0 30.9 %gather_coupled.1 = (bf16[1280,256]{1,0:T(8,128)(2,1)}, bf16[2,7,128,128]{3,2,1,0:T(8,128)(2,1)}) custom-call(bf16[2,1280,896]{2,1,0:T(8,128)(2,1)} %waves.1, bf16[2,64,1280]{2,1,0:T(8,128)(2,1)} %proj.1, f32[12,13,13]{2,1,0:T(8,128)} %coupling.1, s32[12]{0:T(128)} %offsets.1, s32[12]{0:T(128)} %counts.1), custom_call_target="tpu_custom_call" | custom-call | tf_op jit(solution)/shard_map/gather_coupled/pallas_call | solution.py:334
  30.9 4.4 %spread_back.1 = bf16[2,1280,896]{2,1,0:T(8,128)(2,1)} custom-call(bf16[1280,256]{1,0:T(8,128)(2,1)} %get-tuple-element.7.pt, bf16[2,7,128,128]{3,2,1,0:T(8,128)(2,1)} %get-tuple-element.8.c), custom_call_target="tpu_custom_call" | custom-call | tf_op jit(solution)/shard_map/spread_back/pallas_call | solution.py:418

commit v5 on v3

--- a/solution.py
+++ b/solution.py
@@ -11,6 +11,7 @@
 M = 13
 LANES = 128
 SLOT = 16
+SHIFT = 4
 MESH = pl.DeviceIdType.MESH
 
 
@@ -25,15 +26,15 @@
         return lax.broadcasted_iota(jnp.int32, shape, dim)
 
     place = iota((NP, wide), 1)
-    atom, entry = lax.div(place, SLOT), lax.rem(place, SLOT)
+    atom, entry = place >> SHIFT, place & (SLOT - 1)
     start = jnp.full((NP, wide), -wide, jnp.int32)
     count = jnp.zeros((NP, wide), jnp.int32)
     for a in range(atoms):
         start = jnp.where(atom == a, offsets[a], start)
         count = jnp.where(atom == a, counts[a], count)
     select = jnp.where((iota((NP, wide), 0) == start + entry) & (entry < count), 1.0, 0.0)
-    repeat = jnp.where(lax.rem(iota((LANES, wide), 1), SLOT) == iota((LANES, wide), 0), 1.0, 0.0)
-    same = lax.div(iota((wide, wide), 0), SLOT) == lax.div(iota((wide, wide), 1), SLOT)
+    repeat = jnp.where((iota((LANES, wide), 1) & (SLOT - 1)) == iota((LANES, wide), 0), 1.0, 0.0)
+    same = (iota((wide, wide), 0) >> SHIFT) == (iota((wide, wide), 1) >> SHIFT)
     spread = dot_exact(spare[...], repeat, 0)
     spread = jnp.where(same, spread, 0.0)
     raw = dot_exact(dot_exact(select, spread, 0), select, 1)
@@ -62,9 +63,9 @@
     return [(first, end - first) for first, end in zip([0] + ends[:-1], ends)]
 
 
-def gather_kernel(n_pw, n_band, waves, proj, coupling, offsets, counts, pt_out, c_out,
+def gather_kernel(n_pw, n_band, waves, proj, coupling_in, offsets_in, counts_in, pt_out, c_out,
                   w, p_all, acc, sib, send, recv, last_send, last_recv, total, c_all, pt, spare, block,
-                  w_sem, own_sem, out_sem, p_send, p_recv, s_send, s_recv,
+                  coupling, offsets, counts, small_sem, w_sem, own_sem, out_sem, p_send, p_recv, s_send, s_recv,
                   r_send, r_recv, l_send, l_recv, g_send, g_recv, f_send, f_recv, h_send, h_recv):
     pw = lax.axis_index("pw")
     band = lax.axis_index("band")
@@ -103,6 +104,10 @@
     own_rows = pl.multiple_of(band * held, held)
     own = pltpu.make_async_copy(proj, p_all.at[:, pl.ds(own_rows, held), :], own_sem.at[0])
     own.start()
+    small = [pltpu.make_async_copy(source, target, small_sem.at[i]) for i, (source, target) in enumerate(
+        [(coupling_in, coupling), (offsets_in, offsets), (counts_in, counts)])]
+    for copy in small:
+        copy.start()
     wave_copies = []
     for t, (start, size) in enumerate(tiles):
         copy = pltpu.make_async_copy(
@@ -115,6 +120,10 @@
         pl.semaphore_signal(barrier, inc=1, device_id=(pw_at(d), band), device_id_type=MESH)
     for d in range(1, n_band):
         pl.semaphore_signal(barrier, inc=1, device_id=(pw, lax.rem(band + d, n_band)), device_id_type=MESH)
+    for copy in small:
+        copy.wait()
+    block[...] = coupling_block(coupling, offsets, counts, spare)
+    total[...] = jnp.zeros_like(total)
     pl.semaphore_wait(barrier, n_band - 1 + n_pw - 1)
 
     p_copies = []
@@ -262,9 +271,7 @@
     project(0)
     if last > 0:
         sibling_copy(0).start()
-        total[...] = jnp.zeros_like(total)
         reduce_send(0)
-    block[...] = coupling_block(coupling, offsets, counts, spare)
     for i in range(1, last + 1):
         p_copies[i - 1].wait_recv()
         project(i)
@@ -281,12 +288,6 @@
     pt[:, NP:] = p_all[1].T
     pt_copy = pltpu.make_async_copy(pt, pt_out, out_sem.at[0])
     pt_copy.start()
-    for copy in p_copies:
-        copy.wait_send()
-    for i in range(last):
-        sibling_copy(i).wait_send()
-        for d in range(1, chips):
-            pl.when(chip_at(d) < blocks)(lambda: reduce_copy(i, d).wait_send())
 
     pl.when(owns)(lambda: couple(last))
     for i in early:
@@ -295,6 +296,12 @@
         for b in range(blocks):
             forward_copy(i, 1 - core, b).wait_recv()
         out_copy(i).start()
+    for copy in p_copies:
+        copy.wait_send()
+    for i in range(last):
+        sibling_copy(i).wait_send()
+        for d in range(1, chips):
+            pl.when(chip_at(d) < blocks)(lambda: reduce_copy(i, d).wait_send())
     for e in range(1, n_pw):
         pl.when(lax.div(pw_at(e), 2) < blocks)(lambda: final_copy(pw_at(e), e).wait_recv())
     out_copy(last).start()
@@ -328,9 +335,7 @@
     last_rows = sizes[-1]
     bf16, f32 = jnp.bfloat16, jnp.float32
     dma = pltpu.SemaphoreType.DMA
-    hbm = pl.BlockSpec(memory_space=pltpu.HBM)
     anywhere = pl.BlockSpec(memory_space=pl.ANY)
-    scalars = pl.BlockSpec(memory_space=pltpu.SMEM)
     wide = -(-coupling.shape[0] * SLOT // LANES) * LANES
     return pl.pallas_call(
         functools.partial(gather_kernel, n_pw, n_band),
@@ -338,7 +343,7 @@
             jax.ShapeDtypeStruct((depth, 2 * NP), bf16),
             jax.ShapeDtypeStruct((2, blocks, NP, LANES), bf16),
         ],
-        in_specs=[hbm, hbm, pl.BlockSpec(memory_space=pltpu.VMEM), scalars, scalars],
+        in_specs=[anywhere] * 5,
         out_specs=[anywhere, anywhere],
         scratch_shapes=[
             pltpu.VMEM((2, depth, columns), bf16),
@@ -354,6 +359,10 @@
             pltpu.VMEM((depth, 2 * NP), bf16),
             pltpu.VMEM((wide, LANES), f32),
             pltpu.VMEM((NP, NP), f32),
+            pltpu.VMEM(coupling.shape, f32),
+            pltpu.SMEM(offsets.shape, jnp.int32),
+            pltpu.SMEM(counts.shape, jnp.int32),
+            dma((3,)),
             dma((len(column_tiles(columns)),)), dma((1,)), dma((1 + pieces,)),
             dma((n_band - 1, subs)), dma((n_band - 1, subs)),
             dma((pieces,)), dma((pieces,)),
@@ -370,7 +379,7 @@
 
 
 def row_parts(depth):
-    ends = list(range(512, depth, 512)) + [depth]
+    ends = list(range(768, depth, 768)) + [depth]
     return [(first, end - first) for first, end in zip([0] + ends[:-1], ends)]
 
 

time: 34.9 us -> 34.4 us (0.986)
  Pallas kernels: 34.4 us -> 33.9 us
    pallas_call x1, Pallas kernels: 30.3 us -> 29.6 us  [gather_coupled(): pl.pallas_call(functools.partial(gather_kernel, n_pw, n_band), out_shape=...]
where the time goes in v5:
time: 34.4 us; the launch traced here: 33.9 us
  Pallas kernels  33.9 us (99%)
    pallas_call x1, Pallas kernels, gather_coupled(): pl.pallas_call(functools.partial(gather_kernel, n_pw, n_band), out_shape=...  29.6 us
    pallas_call x1, Pallas kernels, spread_back(): pl.pallas_call(spread_kernel, out_shape=jax.ShapeDtypeStruct((2, depth, b...  4.28 us

profile of v5, /device:TPU:1, one launch (start us, length us, event | category | flops | bytes accessed | tf_op | source)
XLA Modules:
  0.0 33.9 jit_solution(3478857937514705232)
XLA Ops:
  0.0 29.6 %gather_coupled.1 = (bf16[1280,256]{1,0:T(8,128)(2,1)}, bf16[2,7,128,128]{3,2,1,0:T(8,128)(2,1)}) custom-call(bf16[2,1280,896]{2,1,0:T(8,128)(2,1)} %waves.1, bf16[2,64,1280]{2,1,0:T(8,128)(2,1)} %proj.1, f32[12,13,13]{2,1,0:T(8,128)} %coupling_in.1, s32[12]{0:T(128)} %offsets_in.1, s32[12]{0:T(128)} %counts_in.1), custom_call_target="tpu_custom_call" | custom-call | tf_op jit(solution)/shard_map/gather_coupled/pallas_call | solution.py:340
  29.6 4.3 %spread_back.1 = bf16[2,1280,896]{2,1,0:T(8,128)(2,1)} custom-call(bf16[1280,256]{1,0:T(8,128)(2,1)} %get-tuple-element.7.pt, bf16[2,7,128,128]{3,2,1,0:T(8,128)(2,1)} %get-tuple-element.8.c), custom_call_target="tpu_custom_call" | custom-call | tf_op jit(solution)/shard_map/spread_back/pallas_call | solution.py:428

commit v6 on v5

--- a/solution.py
+++ b/solution.py
@@ -66,7 +66,7 @@
 def gather_kernel(n_pw, n_band, waves, proj, coupling_in, offsets_in, counts_in, pt_out, c_out,
                   w, p_all, acc, sib, send, recv, last_send, last_recv, total, c_all, pt, spare, block,
                   coupling, offsets, counts, small_sem, w_sem, own_sem, out_sem, p_send, p_recv, s_send, s_recv,
-                  r_send, r_recv, l_send, l_recv, g_send, g_recv, f_send, f_recv, h_send, h_recv):
+                  r_send, r_recv, l_send, l_recv, g_send, g_recv, y_send, f_send, f_recv, h_send, h_recv):
     pw = lax.axis_index("pw")
     band = lax.axis_index("band")
     chip, core = lax.div(pw, 2), lax.rem(pw, 2)
@@ -85,6 +85,13 @@
 
     def pw_at(step):
         return lax.rem(pw + step, n_pw)
+
+    side = 4 if chips % 4 == 0 else 1
+    across = chips // side
+
+    def chip_of(dz, dy):
+        z, y = lax.div(chip, across), lax.rem(chip, across)
+        return lax.rem(z + dz, side) * across + lax.rem(y + dy, across)
 
     def same_core(other):
         return (other * 2 + core, band)
@@ -198,12 +205,19 @@
             send_sem=l_send.at[e], recv_sem=l_recv.at[pw],
             device_id=(target, band), device_id_type=MESH)
 
-    def gather_copy(i, b, d):
+    def line_copy(i, b, dz):
         rows = window(i)
         return pltpu.make_async_remote_copy(
             src_ref=c_all.at[core, b, rows, :], dst_ref=c_all.at[core, b, rows, :],
-            send_sem=g_send.at[i, d], recv_sem=g_recv.at[i, b],
-            device_id=same_core(chip_at(d)), device_id_type=MESH)
+            send_sem=g_send.at[i, dz], recv_sem=g_recv.at[i, b],
+            device_id=same_core(chip_of(dz, 0)), device_id_type=MESH)
+
+    def cross_copy(i, b, dy):
+        rows = window(i)
+        return pltpu.make_async_remote_copy(
+            src_ref=c_all.at[core, b, rows, :], dst_ref=c_all.at[core, b, rows, :],
+            send_sem=y_send.at[i, b, dy], recv_sem=g_recv.at[i, b],
+            device_id=same_core(chip_of(0, dy)), device_id_type=MESH)
 
     def forward_copy(i, k, b):
         rows = window(i)
@@ -246,18 +260,32 @@
             for e in range(1, n_pw):
                 final_copy(pw, e).start()
         else:
-            for d in range(1, chips):
-                gather_copy(i, chip, d).start()
+            for dz in range(1, side):
+                line_copy(i, chip, dz).start()
+            for dy in range(1, across):
+                cross_copy(i, chip, dy).start()
             forward_copy(i, core, chip).start()
 
-    def forward(i):
-        for d in range(1, chips):
-            source = chip_at(d)
+    def forward_line(i):
+        for dz in range(1, side):
+            source = chip_of(dz, 0)
 
             @pl.when(source < blocks)
             def _():
-                gather_copy(i, source, d).wait_recv()
+                line_copy(i, source, dz).wait_recv()
+                for dy in range(1, across):
+                    cross_copy(i, source, dy).start()
                 forward_copy(i, core, source).start()
+
+    def forward_cross(i):
+        for dz in range(side):
+            for dy in range(1, across):
+                source = chip_of(dz, dy)
+
+                @pl.when(source < blocks)
+                def _():
+                    cross_copy(i, source, dy).wait_recv()
+                    forward_copy(i, core, source).start()
 
     def out_copy(i):
         rows = window(i)
@@ -291,7 +319,9 @@
 
     pl.when(owns)(lambda: couple(last))
     for i in early:
-        forward(i)
+        forward_line(i)
+    for i in early:
+        forward_cross(i)
     for i in early:
         for b in range(blocks):
             forward_copy(i, 1 - core, b).wait_recv()
@@ -312,13 +342,19 @@
     @pl.when(owns)
     def _():
         for i in early:
-            for d in range(1, chips):
-                gather_copy(i, chip, d).wait_send()
+            for dz in range(1, side):
+                line_copy(i, chip, dz).wait_send()
+            for dy in range(1, across):
+                cross_copy(i, chip, dy).wait_send()
         for e in range(1, n_pw):
             final_copy(pw, e).wait_send()
     for i in early:
         for b in range(blocks):
             forward_copy(i, core, b).wait_send()
+        for dz in range(1, side):
+            source = chip_of(dz, 0)
+            for dy in range(1, across):
+                pl.when(source < blocks)(lambda: cross_copy(i, source, dy).wait_send())
         out_copy(i).wait()
     pt_copy.wait()
     out_copy(last).wait()
@@ -368,7 +404,7 @@
             dma((pieces,)), dma((pieces,)),
             dma((pieces, chips)), dma((pieces, chips)),
             dma((n_pw,)), dma((n_pw,)),
-            dma((pieces, chips)), dma((pieces, blocks)),
+            dma((pieces, chips)), dma((pieces, blocks)), dma((pieces, blocks, chips)),
             dma((pieces, blocks)), dma((pieces, blocks)),
             dma((n_pw,)), dma((n_pw,)),
         ],
@@ -379,7 +415,7 @@
 
 
 def row_parts(depth):
-    ends = list(range(768, depth, 768)) + [depth]
+    ends = list(range(512, depth, 512)) + [depth]
     return [(first, end - first) for first, end in zip([0] + ends[:-1], ends)]
 
 

time: 34.4 us -> 35.2 us (1.023); the launches traced: 33.9 us -> 35.1 us
  Pallas kernels: 33.9 us -> 35.1 us
    pallas_call x1, Pallas kernels: 29.6 us -> 30.9 us  [gather_coupled(): pl.pallas_call(functools.partial(gather_kernel, n_pw, n_band), out_shape=...]
where the time goes in v6:
time: 35.2 us; the launch traced here: 35.1 us
  Pallas kernels  35.1 us (100%)
    pallas_call x1, Pallas kernels, gather_coupled(): pl.pallas_call(functools.partial(gather_kernel, n_pw, n_band), out_shape=...  30.9 us
    pallas_call x1, Pallas kernels, spread_back(): pl.pallas_call(spread_kernel, out_shape=jax.ShapeDtypeStruct((2, depth, b...  4.14 us

profile of v6, /device:TPU:1, one launch (start us, length us, event | category | flops | bytes accessed | tf_op | source)
XLA Modules:
  0.0 35.1 jit_solution(17406947721971000680)
XLA Ops:
  0.0 30.9 %gather_coupled.1 = (bf16[1280,256]{1,0:T(8,128)(2,1)}, bf16[2,7,128,128]{3,2,1,0:T(8,128)(2,1)}) custom-call(bf16[2,1280,896]{2,1,0:T(8,128)(2,1)} %waves.1, bf16[2,64,1280]{2,1,0:T(8,128)(2,1)} %proj.1, f32[12,13,13]{2,1,0:T(8,128)} %coupling_in.1, s32[12]{0:T(128)} %offsets_in.1, s32[12]{0:T(128)} %counts_in.1), custom_call_target="tpu_custom_call" | custom-call | tf_op jit(solution)/shard_map/gather_coupled/pallas_call | solution.py:376
  30.9 4.1 %spread_back.1 = bf16[2,1280,896]{2,1,0:T(8,128)(2,1)} custom-call(bf16[1280,256]{1,0:T(8,128)(2,1)} %get-tuple-element.7.pt, bf16[2,7,128,128]{3,2,1,0:T(8,128)(2,1)} %get-tuple-element.8.c), custom_call_target="tpu_custom_call" | custom-call | tf_op jit(solution)/shard_map/spread_back/pallas_call | solution.py:464

commit v7 on v5

--- a/solution.py
+++ b/solution.py
@@ -303,10 +303,6 @@
         for d in range(1, chips):
             pl.when(chip_at(d) < blocks)(lambda: reduce_copy(i, d).wait_send())
     for e in range(1, n_pw):
-        pl.when(lax.div(pw_at(e), 2) < blocks)(lambda: final_copy(pw_at(e), e).wait_recv())
-    out_copy(last).start()
-
-    for e in range(1, n_pw):
         pl.when(lax.div(pw_at(e), 2) < blocks)(lambda: last_copy(e).wait_send())
 
     @pl.when(owns)
@@ -319,8 +315,12 @@
     for i in early:
         for b in range(blocks):
             forward_copy(i, core, b).wait_send()
+    for e in range(1, n_pw):
+        pl.when(lax.div(pw_at(e), 2) < blocks)(lambda: final_copy(pw_at(e), e).wait_recv())
+    out_copy(last).start()
+    pt_copy.wait()
+    for i in early:
         out_copy(i).wait()
-    pt_copy.wait()
     out_copy(last).wait()
 
 
@@ -379,7 +379,7 @@
 
 
 def row_parts(depth):
-    ends = list(range(768, depth, 768)) + [depth]
+    ends = list(range(512, depth, 512)) + [depth]
     return [(first, end - first) for first, end in zip([0] + ends[:-1], ends)]
 
 

time: 34.4 us -> 34.2 us (level)
  no operation moved by 1% of the time
where the time goes in v7:
time: 34.2 us; the launch traced here: 33.8 us
  Pallas kernels  33.7 us (99%)
    pallas_call x1, Pallas kernels, gather_coupled(): pl.pallas_call(functools.partial(gather_kernel, n_pw, n_band), out_shape=...  29.6 us
    pallas_call x1, Pallas kernels, spread_back(): pl.pallas_call(spread_kernel, out_shape=jax.ShapeDtypeStruct((2, depth, b...  4.14 us

profile of v7, /device:TPU:1, one launch (start us, length us, event | category | flops | bytes accessed | tf_op | source)
XLA Modules:
  0.0 33.8 jit_solution(6814680561458098439)
XLA Ops:
  0.0 29.6 %gather_coupled.1 = (bf16[1280,256]{1,0:T(8,128)(2,1)}, bf16[2,7,128,128]{3,2,1,0:T(8,128)(2,1)}) custom-call(bf16[2,1280,896]{2,1,0:T(8,128)(2,1)} %waves.1, bf16[2,64,1280]{2,1,0:T(8,128)(2,1)} %proj.1, f32[12,13,13]{2,1,0:T(8,128)} %coupling_in.1, s32[12]{0:T(128)} %offsets_in.1, s32[12]{0:T(128)} %counts_in.1), custom_call_target="tpu_custom_call" | custom-call | tf_op jit(solution)/shard_map/gather_coupled/pallas_call | solution.py:340
  29.6 4.1 %spread_back.1 = bf16[2,1280,896]{2,1,0:T(8,128)(2,1)} custom-call(bf16[1280,256]{1,0:T(8,128)(2,1)} %get-tuple-element.7.pt, bf16[2,7,128,128]{3,2,1,0:T(8,128)(2,1)} %get-tuple-element.8.c), custom_call_target="tpu_custom_call" | custom-call | tf_op jit(solution)/shard_map/spread_back/pallas_call | solution.py:428

commit v8 on v7

--- a/solution.py
+++ b/solution.py
@@ -144,6 +144,8 @@
         for s, size in enumerate(sizes):
             pieces.append((pl.multiple_of(source * held + sub_row(source, s), SLOT), size))
     last = len(pieces) - 1
+    early = [i for i in range(min(1, last)) if windows[i] is not None]
+    direct = [i for i in range(last + 1) if windows[i] is not None and i not in early]
 
     def project(i):
         row, size = pieces[i]
@@ -212,10 +214,10 @@
             send_sem=f_send.at[i, b], recv_sem=f_recv.at[i, b],
             device_id=sibling, device_id_type=MESH)
 
-    def final_copy(owner, e):
-        here = c_all.at[lax.rem(owner, 2), lax.min(lax.div(owner, 2), blocks - 1), window(last), :]
-        return pltpu.make_async_remote_copy(
-            src_ref=here, dst_ref=here, send_sem=h_send.at[e], recv_sem=h_recv.at[owner],
+    def final_copy(i, owner, e):
+        here = c_all.at[lax.rem(owner, 2), lax.min(lax.div(owner, 2), blocks - 1), window(i), :]
+        return pltpu.make_async_remote_copy(
+            src_ref=here, dst_ref=here, send_sem=h_send.at[i, e], recv_sem=h_recv.at[i, owner],
             device_id=(pw_at(e), band), device_id_type=MESH)
 
     def couple(i):
@@ -242,9 +244,9 @@
         if windows[i] is None:
             return
         c_all[core, chip, window(i), :] = dot_exact(block[window(i), :], total[...], 0).astype(bf16)
-        if i == last:
+        if i in direct:
             for e in range(1, n_pw):
-                final_copy(pw, e).start()
+                final_copy(i, pw, e).start()
         else:
             for d in range(1, chips):
                 gather_copy(i, chip, d).start()
@@ -264,7 +266,6 @@
         return pltpu.make_async_copy(
             c_all.at[:, :, rows, :], c_out.at[:, :, rows, :], out_sem.at[i + 1])
 
-    early = [i for i in range(last) if windows[i] is not None]
     owns = chip < blocks
 
     own.wait()
@@ -311,17 +312,18 @@
             for d in range(1, chips):
                 gather_copy(i, chip, d).wait_send()
         for e in range(1, n_pw):
-            final_copy(pw, e).wait_send()
+            for i in direct:
+                final_copy(i, pw, e).wait_send()
     for i in early:
         for b in range(blocks):
             forward_copy(i, core, b).wait_send()
-    for e in range(1, n_pw):
-        pl.when(lax.div(pw_at(e), 2) < blocks)(lambda: final_copy(pw_at(e), e).wait_recv())
-    out_copy(last).start()
+    for i in direct:
+        for e in range(1, n_pw):
+            pl.when(lax.div(pw_at(e), 2) < blocks)(lambda: final_copy(i, pw_at(e), e).wait_recv())
+        out_copy(i).start()
     pt_copy.wait()
-    for i in early:
+    for i in early + direct:
         out_copy(i).wait()
-    out_copy(last).wait()
 
 
 def gather_coupled(n_pw, n_band, waves, projectors, coupling, offsets, counts):
@@ -370,7 +372,7 @@
             dma((n_pw,)), dma((n_pw,)),
             dma((pieces, chips)), dma((pieces, blocks)),
             dma((pieces, blocks)), dma((pieces, blocks)),
-            dma((n_pw,)), dma((n_pw,)),
+            dma((pieces, n_pw)), dma((pieces, n_pw)),
         ],
         compiler_params=pltpu.CompilerParams(
             collective_id=0, has_side_effects=True, vmem_limit_bytes=60 * 2**20),

time: 34.2 us -> 36.9 us (1.079)
  Pallas kernels: 33.7 us -> 36.4 us
    pallas_call x1, Pallas kernels: 29.6 us -> 32.3 us  [gather_coupled(): pl.pallas_call(functools.partial(gather_kernel, n_pw, n_band), out_shape=...]
where the time goes in v8:
time: 36.9 us; the launch traced here: 36.4 us
  Pallas kernels  36.4 us (99%)
    pallas_call x1, Pallas kernels, gather_coupled(): pl.pallas_call(functools.partial(gather_kernel, n_pw, n_band), out_shape=...  32.3 us
    pallas_call x1, Pallas kernels, spread_back(): pl.pallas_call(spread_kernel, out_shape=jax.ShapeDtypeStruct((2, depth, b...  4.14 us

profile of v8, /device:TPU:1, one launch (start us, length us, event | category | flops | bytes accessed | tf_op | source)
XLA Modules:
  0.0 36.4 jit_solution(16779864433253765803)
XLA Ops:
  0.0 32.3 %gather_coupled.1 = (bf16[1280,256]{1,0:T(8,128)(2,1)}, bf16[2,7,128,128]{3,2,1,0:T(8,128)(2,1)}) custom-call(bf16[2,1280,896]{2,1,0:T(8,128)(2,1)} %waves.1, bf16[2,64,1280]{2,1,0:T(8,128)(2,1)} %proj.1, f32[12,13,13]{2,1,0:T(8,128)} %coupling_in.1, s32[12]{0:T(128)} %offsets_in.1, s32[12]{0:T(128)} %counts_in.1), custom_call_target="tpu_custom_call" | custom-call | tf_op jit(solution)/shard_map/gather_coupled/pallas_call | solution.py:342
  32.3 4.1 %spread_back.1 = bf16[2,1280,896]{2,1,0:T(8,128)(2,1)} custom-call(bf16[1280,256]{1,0:T(8,128)(2,1)} %get-tuple-element.7.pt, bf16[2,7,128,128]{3,2,1,0:T(8,128)(2,1)} %get-tuple-element.8.c), custom_call_target="tpu_custom_call" | custom-call | tf_op jit(solution)/shard_map/spread_back/pallas_call | solution.py:430
